TPU v7x, 256 devices: a whole 4x4x8 slice. The times are simulated.
256 devices in a mesh: rep: 64 (over x_lo, z, y), fsdp: 4 (over x_hi, core).
Axes of the slice: x: 4 (x_hi: 2, x_lo: 2; x = x_hi * 2 + x_lo), y: 4, z: 8, core: 2. Of those that a mesh axis runs over, the one named last changes fastest.
Arguments:
- weight: bfloat16 [64, 4096, 512], P('rep', 'fsdp'), may hold values from -6 to 6
- adam_first: bfloat16 [64, 4096, 512], P('rep', 'fsdp'), may hold values from -3.0517578e-05 to 3.0517578e-05
- adam_second: bfloat16 [64, 4096, 512], P('rep', 'fsdp'), may hold values from 4.7464255e-12 to 4.7521098e-11
- anchor: bfloat16 [4096, 512], P('fsdp'), may hold values from -6 to 6
- momentum: float32 [4096, 512], P('fsdp'), may hold values from -6 to 6
- tokens: bfloat16 [64, 1536, 4096], P('rep', 'fsdp'), may hold values from -20 to 20
- cotangent: bfloat16 [64, 1536, 512], P('rep', 'fsdp'), may hold values from -12 to 12
- plan: int32 [512], P('fsdp'), may hold values from 0 to 1
- mix_weights: float32 [4], replicated, may hold values from 0.2 to 0.8
- mix_index: int32 [64], P('rep'), may hold values from 0 to 3
Outputs:
- new_weight: bfloat16 [64, 4096, 512], P('rep', 'fsdp')
- new_momentum: float32 [4096, 512], P('fsdp')
All inputs are finite; a program needn't handle non-finite values.
Results may differ from a plain program's by a relative error of at most 0.0054.
Values may be sent and summed in bfloat16 or wider, within the bound.
A program may use at most 128 MiB of HBM per device.

v0:
```python
import jax
import jax.numpy as jnp
from jax import lax
from jax.sharding import PartitionSpec as P

HD = 128
FRAG = 2
ROWS = 8


EPS_NORM = 1e-06
BETA_ONE = 0.9
BETA_TWO = 0.999
ADAM_EPS = 1e-08
LEARN_RATE = 0.3
DECAY = 0.1
CLIP = 0.05
MOMENT_COEF = 0.9
OUTER_RATE = 0.7


def head_norm(keys):
    heads = keys.reshape(keys.shape[0], -1, HD)
    factor = lax.rsqrt(jnp.mean(heads * heads, axis=-1, keepdims=True) + EPS_NORM)
    return (heads * factor).reshape(keys.shape)


def key_cotangent(keys, cot):
    _, pullback = jax.vjp(head_norm, keys)
    return pullback(cot.astype(jnp.float32))[0].astype(jnp.bfloat16)


def pick_part(values, row_frag, width):
    picked = jnp.zeros((values.shape[0], width), values.dtype)
    for index in range(FRAG):
        picked = jnp.where(
            row_frag == index, values[:, index * width : (index + 1) * width], picked
        )
    return picked


def place_part(values, update, row_frag, width):
    pieces = []
    for index in range(FRAG):
        pieces.append(
            jnp.where(row_frag == index, update, values[:, index * width : (index + 1) * width])
        )
    return jnp.concatenate(pieces, axis=1)


def replica_mean(anchor, shard, row_frag, width):
    delta = anchor.astype(jnp.float32) - shard.astype(jnp.float32)
    piece = pick_part(delta, row_frag, width)
    return lax.psum(piece, "rep") / lax.axis_size("rep")


def local(
    weight,
    adam_first,
    adam_second,
    anchor,
    momentum,
    tokens,
    cotangent,
    plan,
    mix_weights,
    mix_index,
):
    shard = weight[0]
    inputs = tokens[0]
    cot = cotangent[0]
    columns = shard.shape[1]
    width = columns // FRAG
    row_frag = jnp.repeat(plan, ROWS)[:, None]
    alpha = mix_weights[mix_index[0]]
    features = inputs
    keys = jnp.dot(
        features,
        lax.all_gather(shard, "fsdp", axis=0, tiled=True),
        preferred_element_type=jnp.float32,
    )
    dkeys = key_cotangent(keys, cot)
    features = inputs
    summed = lax.psum_scatter(
        lax.dot_general(
            features, dkeys, (((0,), (0,)), ((), ())), preferred_element_type=jnp.float32
        ).astype(jnp.bfloat16),
        "fsdp",
        scatter_dimension=0,
        tiled=True,
    ).astype(jnp.float32)
    total_tokens = inputs.shape[0] * lax.axis_size("fsdp")
    grad = summed / total_tokens
    squares = lax.psum(jnp.sum(grad * grad), "fsdp")
    clipped = grad * jnp.minimum(1.0, CLIP / jnp.sqrt(squares + 1e-12))
    first = BETA_ONE * adam_first[0].astype(jnp.float32) + (1.0 - BETA_ONE) * clipped
    second = BETA_TWO * adam_second[0].astype(jnp.float32) + (1.0 - BETA_TWO) * clipped * clipped
    wide = shard.astype(jnp.float32)
    inner = wide - LEARN_RATE * (first / (jnp.sqrt(second) + ADAM_EPS) + DECAY * wide)
    average = replica_mean(anchor, shard, row_frag, width)
    old_moment = pick_part(momentum, row_frag, width)
    moved = MOMENT_COEF * old_moment + average
    base = pick_part(anchor, row_frag, width).astype(jnp.float32)
    outer = base - OUTER_RATE * (average + MOMENT_COEF * moved)
    inner_piece = pick_part(inner, row_frag, width)
    blended = alpha * inner_piece + (1.0 - alpha) * outer
    new_weight = place_part(inner, blended, row_frag, width).astype(jnp.bfloat16)[None]
    new_momentum = place_part(momentum, moved, row_frag, width)
    return (new_weight, new_momentum)


def solution(mesh):
    placed = (
        P("rep", "fsdp", None),
        P("rep", "fsdp", None),
        P("rep", "fsdp", None),
        P("fsdp", None),
        P("fsdp", None),
        P("rep", "fsdp", None),
        P("rep", "fsdp", None),
        P("fsdp"),
        P(),
        P("rep"),
    )
    return jax.shard_map(
        local,
        mesh=mesh,
        in_specs=placed,
        out_specs=(P("rep", "fsdp", None), P("fsdp", None)),
        check_vma=False,
    )
```

profile of v0, /device:TPU:4, one launch (start us, length us, event | category | flops | bytes accessed | tf_op | source)
XLA Modules:
  0.0 772.4 jit_solution(5784210387884619601)
XLA Ops:
  7.2 0.0 copy-start
  7.2 0.0 all-gather.3.cloned.1.call-start
  7.2 0.7 all-gather.3.cloned.1.call-update
  7.9 0.0 reduce-scatter.2.cloned.1.call-start
  8.0 2.2 copy.26
  10.2 41.0 %all-gather.3.cloned.1.call-done = bf16[1,4096,512]{2,1,0:T(8,128)(2,1)} async-done(((bf16[1,1024,512]{2,1,0:T(8,128)(2,1)}), bf16[1,4096,512]{2,1,0:T(8,128)(2,1)}) %all-gather.3.cloned.1.call-update) | async-done | bytes 4194320 | tf_op jit(solution)/shard_map/all_gather | solution.py:79
  51.2 6.5 copy.27
  57.7 0.0 copy-done
  57.7 0.0 copy-start.1
  57.7 4.8 multiply_reduce_fusion.1
  62.5 0.0 copy-done.1
  62.5 0.1 fusion.15
  62.7 4.3 fusion
  67.0 0.0 reduce-scatter.2.cloned.1.call-update
  67.0 0.0 all-reduce.2.cloned.1.call-start
  67.0 2.3 copy.24
  69.3 2.3 copy.29
  71.6 0.0 copy-start.2
  71.6 2.3 copy.25
  73.9 2.3 copy.28
  76.1 0.0 copy-done.2
  76.1 0.1 broadcast_in_dim.61
  76.2 0.1 eq.37
  76.3 46.8 %reduce-scatter.2.cloned.1.call-done = bf16[1024,512]{0,1:T(8,128)(2,1)} async-done(((bf16[4096,512]{0,1:T(8,128)(2,1)}), bf16[1024,512]{0,1:T(8,128)(2,1)}) %reduce-scatter.2.cloned.1.call-update) | async-done | bytes 1048592 | tf_op jit(solution)/shard_map/reduce_scatter | solution.py:84
  123.2 2.4 fusion.10
  125.6 0.1 broadcast_in_dim.59
  125.7 0.1 eq.35
  125.8 10.7 %psum.14 = f32[]{:T(128)} all-reduce(f32[]{:T(128)} %fusion.10), channel_id=1, replica_groups=mesh['rep'=64,'fsdp'=4] {'fsdp'}, use_global_device_ids=true, to_apply=%region_4.0 | all-reduce | flops 1 | bytes 8 | tf_op jit(solution)/shard_map/psum | solution.py:94
  137.2 5.7 convert_subtract_fusion
  142.9 1.2 fusion.14
  144.1 0.0 all-reduce.2.cloned.1.call-update
  144.2 3.0 fusion.20
  147.2 0.0 copy-start.3
  147.2 2.6 copy.36
  149.7 2.6 copy.37
  153.0 0.0 copy-done.3
  153.0 0.7 dynamic_slice.3
  154.3 595.8 %all-reduce.2.cloned.1.call-done = f32[1024,256]{0,1:T(8,128)} async-done(((f32[1024,256]{0,1:T(8,128)}), f32[1024,256]{0,1:T(8,128)}) %all-reduce.2.cloned.1.call-update) | async-done | bytes 1048592 | tf_op jit(solution)/shard_map/psum | solution.py:54
  750.1 2.2 broadcast_select_fusion.1
  752.3 1.4 pad_maximum_fusion
  753.7 2.9 copy.35
  756.6 4.6 fusion.16
  761.2 1.3 fusion.17
  762.5 1.0 pad_maximum_fusion.1
  763.6 2.3 copy.34
  (2 shorter events, 0.0 us)
Async XLA Ops:
  7.2 50.5 %copy-start = (bf16[1,384,4096]{2,1,0:T(8,128)(2,1)S(1)}, bf16[1,384,4096]{2,1,0:T(8,128)(2,1)}, u32[]{:S(2)}) copy-start(bf16[1,384,4096]{2,1,0:T(8,128)(2,1)} %param.15) | copy-start | bytes 9437188
  7.2 44.0 %all-gather.3.cloned.1.call-start = ((), (), s32[]{:S(2)}) async-start(), calls=%async_computation.3 | async-start | bytes 5242880 | tf_op jit(solution)/shard_map/all_gather | solution.py:79
  7.9 115.3 %reduce-scatter.2.cloned.1.call-start = ((), (), s32[]{:S(2)}) async-start(), calls=%async_computation.1 | async-start | bytes 5242880 | tf_op jit(solution)/shard_map/reduce_scatter | solution.py:84
  57.7 4.9 copy-start.1
  67.0 683.1 %all-reduce.2.cloned.1.call-start = ((), (), s32[]{:S(2)}) async-start(), calls=%async_computation.2 | async-start | bytes 2097152 | tf_op jit(solution)/shard_map/psum | solution.py:54
  71.6 4.6 copy-start.2
  147.2 5.8 copy-start.3
Sparse Core Ops, SparseCore 0:
  9.8 41.3 all-gather.2
  67.1 56.0 reduce-scatter.1
  144.3 605.7 all-reduce.1
where the time goes:
time: 773 us; the launch traced here: 772 us
  waiting for transfers between devices  684 us (88%)
  local copies, waits for them, and re-layouts  32.1 us (4%)
  other arithmetic  20.2 us (3%)
  between operations  15.8 us (2%)
  blocking collectives  10.7 us (1%)
  matrix products  9.11 us (1%)
    psum x1, waiting for transfers between devices, replica_mean(): return lax.psum(piece, 'rep') / lax.axis_size('rep')  596 us
    reduce_scatter x1, waiting for transfers between devices, local(): lax.psum_scatter(lax.dot_general(features, dkeys, (((0,), (0,)), ((), ())...  46.8 us
    all_gather x1, waiting for transfers between devices, local(): lax.all_gather(shard, 'fsdp', axis=0, tiled=True)  41 us
    unnamed x16, local copies, waits for them, and re-layouts  19.4 us
  transfers between devices with their start and end apart: 3, of which 3 were waited for; matrix products, arithmetic and copies ran while one was open for 3% of the time, Pallas kernels for 0%

commit v1 on v0

v1 whole, which is shorter than its diff:
```python
import functools

import jax
import jax.numpy as jnp
from jax import lax
from jax.experimental import pallas as pl
from jax.experimental.pallas import tpu as pltpu
from jax.sharding import PartitionSpec as P

HD = 128
ROWS = 8
EPS_NORM = 1e-06
BETA_ONE = 0.9
BETA_TWO = 0.999
ADAM_EPS = 1e-08
LEARN_RATE = 0.3
DECAY = 0.1
CLIP = 0.05
MOMENT_COEF = 0.9
OUTER_RATE = 0.7

MESH = pl.DeviceIdType.MESH
F32 = jnp.float32
BF16 = jnp.bfloat16

NY = 4
NZ = 8
REPS = 64
TOK = 384
FEAT = 1024
COLS = 512
HALF = 256
PARTS = 4
PROWS = FEAT // PARTS
YROWS = FEAT // NY
ZROWS = YROWS // NZ


def place(x_lo, z, y, f):
    return (x_lo * (NZ * NY) + z * NY + y, f)


def kernel(
    weight,
    adam_first,
    adam_second,
    anchor,
    momentum,
    tokens,
    cotangent,
    plan,
    mix_weights,
    mix_index,
    new_weight,
    new_momentum,
    wown,
    wrecv,
    tch,
    tt,
    cot,
    mask,
    picked,
    yrecv,
    ysum,
    zrecv,
    zsum,
    xrecv,
    mean,
    psend,
    precv,
    dch,
    gsend,
    grecv,
    gown,
    first,
    second,
    base,
    old,
    level,
    factor,
    sq,
    load_sem,
    wsend_sem,
    wrecv_sem,
    tsend_sem,
    trecv_sem,
    ysend_sem,
    yrecv_sem,
    zsend_sem,
    zrecv_sem,
    xsend_sem,
    xrecv_sem,
    azsend_sem,
    azrecv_sem,
    aysend_sem,
    ayrecv_sem,
    psend_sem,
    precv_sem,
    dsend_sem,
    drecv_sem,
    gsend_sem,
    grecv_sem,
    qsend_sem,
    qrecv_sem,
):
    rep = lax.axis_index("rep")
    f = lax.axis_index("fsdp")
    x_lo = rep // (NZ * NY)
    z = (rep // NY) % NZ
    y = rep % NY
    mate_f = f + 1 - 2 * (f % 2)
    across_f = (f + 2) % 4
    diag_f = 3 - f
    mate = (rep, mate_f)
    across = (rep, across_f)
    diag = (rep, diag_f)
    y_peers = [place(x_lo, z, (y + d) % NY, f) for d in range(1, NY)]
    z_peers = [place(x_lo, (z + d) % NZ, y, f) for d in range(1, NZ)]
    x_peer = place(1 - x_lo, z, y, f)

    barrier = pltpu.get_barrier_semaphore()
    peers = [across, mate, diag, x_peer] + y_peers + z_peers
    for peer in peers:
        pl.semaphore_signal(barrier, inc=1, device_id=peer, device_id_type=MESH)

    def columns(index):
        return pl.ds(pl.multiple_of(index * FEAT, FEAT), FEAT)

    loads = [
        pltpu.make_async_copy(weight.at[0], wown, load_sem.at[0]),
        pltpu.make_async_copy(
            tokens.at[0, :, columns(f)], tch.at[0, :, pl.ds(0, FEAT)], load_sem.at[1]
        ),
        pltpu.make_async_copy(
            tokens.at[0, :, columns(across_f)], tch.at[0, :, pl.ds(FEAT, FEAT)], load_sem.at[2]
        ),
        pltpu.make_async_copy(cotangent.at[0], cot, load_sem.at[3]),
        pltpu.make_async_copy(anchor, base, load_sem.at[4]),
        pltpu.make_async_copy(momentum, old, load_sem.at[5]),
        pltpu.make_async_copy(adam_first.at[0], first, load_sem.at[6]),
        pltpu.make_async_copy(adam_second.at[0], second, load_sem.at[7]),
    ]
    for copy in loads:
        copy.start()

    def mark(i, _):
        mask[pl.ds(pl.multiple_of(i * ROWS, ROWS), ROWS), :] = jnp.full((ROWS, HD), plan[i], jnp.int32)
        return 0

    lax.fori_loop(0, FEAT // ROWS, mark, 0, unroll=8)

    pl.semaphore_wait(barrier, len(peers))

    def remote(src, dst, send, recv, to):
        return pltpu.make_async_remote_copy(
            src_ref=src, dst_ref=dst, send_sem=send, recv_sem=recv, device_id=to, device_id_type=MESH
        )

    w_copies = [
        remote(
            weight.at[0, :, pl.ds(j * HALF, HALF)], wrecv.at[j], wsend_sem.at[j], wrecv_sem.at[j], across
        )
        for j in range(2)
    ]
    for copy in w_copies:
        copy.start()
    t_copies = [
        remote(
            tokens.at[0, :, columns(index)],
            tch.at[1, :, pl.ds(b * FEAT, FEAT)],
            tsend_sem.at[b],
            trecv_sem.at[b],
            mate,
        )
        for b, index in enumerate((mate_f, diag_f))
    ]
    for copy in t_copies:
        copy.start()

    loads[0].wait()

    def pick(start):
        def body(i, _):
            rows = pl.ds(pl.multiple_of(start + i * 32, 32), 32)
            chosen = mask[rows, :] == 0
            for k in range(HALF // HD):
                low = wown[rows, k * HD : (k + 1) * HD].astype(F32)
                high = wown[rows, HALF + k * HD : HALF + (k + 1) * HD].astype(F32)
                picked[rows, k * HD : (k + 1) * HD] = jnp.where(chosen, low, high).astype(BF16)
            return 0

        lax.fori_loop(0, YROWS // 32, body, 0, unroll=2)

    y_copies = []
    for d in range(1, NY):
        start = ((y + d) % NY) * YROWS
        pick(start)
        y_copies.append(
            remote(
                picked.at[pl.ds(pl.multiple_of(start, YROWS), YROWS)],
                yrecv.at[d - 1],
                ysend_sem.at[d - 1],
                yrecv_sem.at[d - 1],
                y_peers[d - 1],
            )
        )
        y_copies[-1].start()
    pick(y * YROWS)

    def turn(t):
        def body(i, _):
            at = pl.multiple_of(i * HD, HD)
            tt[pl.ds(at, HD), t * TOK : (t + 1) * TOK] = tch[t, :, pl.ds(at, HD)].T
            return 0

        lax.fori_loop(0, 2 * FEAT // HD, body, 0)

    loads[1].wait()
    loads[2].wait()
    turn(0)

    for copy in y_copies:
        copy.wait_recv()

    def add_y(i, _):
        at = pl.multiple_of(i * 32, 32)
        rows = pl.ds(at, 32)
        total = picked[pl.ds(pl.multiple_of(y * YROWS + i * 32, 32), 32), :].astype(F32)
        for d in range(NY - 1):
            total = total + yrecv[d, rows, :].astype(F32)
        ysum[rows, :] = total
        return 0

    lax.fori_loop(0, YROWS // 32, add_y, 0)
    z_copies = []
    for d in range(1, NZ):
        start = pl.multiple_of(((z + d) % NZ) * ZROWS, ZROWS)
        z_copies.append(
            remote(
                ysum.at[pl.ds(start, ZROWS)],
                zrecv.at[d - 1],
                zsend_sem.at[d - 1],
                zrecv_sem.at[d - 1],
                z_peers[d - 1],
            )
        )
        z_copies[-1].start()

    for copy in t_copies:
        copy.wait_recv()
    turn(1)
    loads[3].wait()

    own_block = pl.ds(0, FEAT)
    across_block = pl.ds(FEAT, FEAT)
    p_copies = []
    d_copies = []
    g_copies = []

    def project(t, j):
        mine = jnp.dot(
            tch[t, :, own_block], wown[:, j * HALF : (j + 1) * HALF], preferred_element_type=F32
        )
        return mine + jnp.dot(tch[t, :, across_block], wrecv[j], preferred_element_type=F32)

    def chunk(j):
        w_copies[j].wait_recv()
        psend[j] = project(1, j)
        p_copy = remote(psend.at[j], precv.at[j], psend_sem.at[j], precv_sem.at[j], mate)
        p_copy.start()
        p_copies.append(p_copy)
        keys = project(0, j)
        p_copy.wait_recv()
        keys = keys + precv[j]
        for k in range(HALF // HD):
            at = j * HALF + k * HD
            head = keys[:, k * HD : (k + 1) * HD]
            pull = cot[:, at : at + HD].astype(F32)
            scale = lax.rsqrt(jnp.sum(head * head, axis=1, keepdims=True) * (1.0 / HD) + EPS_NORM)
            inner = jnp.sum(head * pull, axis=1, keepdims=True) * (1.0 / HD)
            back = scale * (pull - head * (scale * scale * inner))
            dch[j, 0, :, k * HD : (k + 1) * HD] = back.astype(BF16)
        d_copy = remote(dch.at[j, 0], dch.at[j, 1], dsend_sem.at[j], drecv_sem.at[j], mate)
        d_copy.start()
        d_copies.append(d_copy)
        d_copy.wait_recv()

        def grad(at):
            low = jnp.dot(tt[pl.ds(at, PROWS), 0:TOK], dch[j, 0], preferred_element_type=F32)
            high = jnp.dot(
                tt[pl.ds(at, PROWS), TOK : 2 * TOK], dch[j, 1], preferred_element_type=F32
            )
            return low + high

        for i in range(PARTS):
            gsend[j, i] = grad(FEAT + i * PROWS).astype(BF16)
            g_copy = remote(
                gsend.at[j, i], grecv.at[j, i], gsend_sem.at[j, i], grecv_sem.at[j, i], across
            )
            g_copy.start()
            g_copies.append(g_copy)
        for i in range(PARTS):
            gown[j, i] = grad(i * PROWS)

    chunk(0)

    for copy in z_copies:
        copy.wait_recv()
    total = ysum[pl.ds(pl.multiple_of(z * ZROWS, ZROWS), ZROWS), :]
    for d in range(NZ - 1):
        total = total + zrecv[d]
    zsum[...] = total
    x_copy = remote(zsum, xrecv, xsend_sem, xrecv_sem, x_peer)
    x_copy.start()
    x_copy.wait_recv()
    mine = pl.ds(pl.multiple_of(y * YROWS + z * ZROWS, ZROWS), ZROWS)
    mean[mine, :] = (zsum[...] + xrecv[...]) * (1.0 / REPS)
    az_copies = []
    for d in range(1, NZ):
        az_copies.append(
            remote(
                mean.at[mine], mean.at[mine], azsend_sem.at[d - 1], azrecv_sem.at[d - 1], z_peers[d - 1]
            )
        )
        az_copies[-1].start()

    chunk(1)

    for copy in az_copies:
        copy.wait_recv()
    block = pl.ds(pl.multiple_of(y * YROWS, YROWS), YROWS)
    ay_copies = []
    for d in range(1, NY):
        ay_copies.append(
            remote(
                mean.at[block],
                mean.at[block],
                aysend_sem.at[d - 1],
                ayrecv_sem.at[d - 1],
                y_peers[d - 1],
            )
        )
        ay_copies[-1].start()

    def gather(j, i, total):
        g_copies[j * PARTS + i].wait_recv()

        def body(s, total):
            rows = pl.ds(pl.multiple_of(s * 32, 32), 32)
            grad = (gown[j, i, rows, :] + grecv[j, i, rows, :].astype(F32)) * (1.0 / (4 * TOK))
            gown[j, i, rows, :] = grad
            square = grad * grad
            for r in range(4):
                for k in range(HALF // HD):
                    total = total + square[r * 8 : (r + 1) * 8, k * HD : (k + 1) * HD]
            return total

        return lax.fori_loop(0, PROWS // 32, body, total, unroll=2)

    squares = jnp.zeros((8, HD), F32)
    for i in range(PARTS):
        squares = gather(0, i, squares)

    for copy in loads[4:]:
        copy.wait()
    choice = mix_index[0]
    alpha = mix_weights[0]
    for k in range(1, 4):
        alpha = jnp.where(choice == k, mix_weights[k], alpha)
    for copy in ay_copies:
        copy.wait_recv()

    def outer_step(i, _):
        rows = pl.ds(pl.multiple_of(i * 16, 16), 16)
        row_frag = mask[rows, :]
        for k in range(HALF // HD):
            middle = mean[rows, k * HD : (k + 1) * HD]
            for index in range(2):
                at = index * HALF + k * HD
                chosen = row_frag == index
                start = base[rows, at : at + HD].astype(F32)
                wide = wown[rows, at : at + HD].astype(F32) * (1.0 - LEARN_RATE * DECAY)
                before = old[rows, at : at + HD]
                average = start - middle
                moved = MOMENT_COEF * before + average
                outer = start - OUTER_RATE * (average + MOMENT_COEF * moved)
                new_momentum[rows, at : at + HD] = jnp.where(chosen, moved, before)
                level[rows, at : at + HD] = jnp.where(
                    chosen, alpha * wide + (1.0 - alpha) * outer, wide
                )
        return 0

    lax.fori_loop(0, FEAT // 16, outer_step, 0)

    for i in range(PARTS):
        squares = gather(1, i, squares)
    sq[0] = squares
    q_copies = []
    for d, peer in enumerate((mate, across, diag)):
        q_copies.append(remote(sq.at[0], sq.at[1 + d], qsend_sem.at[d], qrecv_sem.at[d], peer))
        q_copies[-1].start()
    for copy in q_copies:
        copy.wait_recv()
    everything = jnp.sum(sq[0] + sq[1] + sq[2] + sq[3], keepdims=True)
    clip = jnp.minimum(1.0, CLIP / jnp.sqrt(everything + 1e-12))
    factor[...] = jnp.broadcast_to(clip, (8, HD))

    for j in range(2):
        for i in range(PARTS):

            def adam(s, _, j=j, i=i):
                at = pl.multiple_of(s * 16, 16)
                rows = pl.ds(pl.multiple_of(i * PROWS + s * 16, 16), 16)
                ratio = jnp.concatenate([factor[...]] * 2, axis=0)
                chosen_row = mask[rows, :]
                rate = jnp.where(chosen_row == j, alpha * LEARN_RATE, LEARN_RATE)
                for k in range(HALF // HD):
                    c = j * HALF + k * HD
                    clipped = gown[j, i, pl.ds(at, 16), k * HD : (k + 1) * HD] * ratio
                    one = BETA_ONE * first[rows, c : c + HD].astype(F32) + (1.0 - BETA_ONE) * clipped
                    two = (
                        BETA_TWO * second[rows, c : c + HD].astype(F32)
                        + (1.0 - BETA_TWO) * clipped * clipped
                    )
                    step = one / (jnp.sqrt(two) + ADAM_EPS)
                    new_weight[0, rows, c : c + HD] = (
                        level[rows, c : c + HD] - rate * step
                    ).astype(BF16)
                return 0

            lax.fori_loop(0, PROWS // 16, adam, 0, unroll=4)

    sent = w_copies + t_copies + y_copies + z_copies + [x_copy] + az_copies + ay_copies
    for copy in sent + p_copies + d_copies + g_copies + q_copies:
        copy.wait_send()


def local(*args):
    dma = pltpu.SemaphoreType.DMA
    any_space = pl.BlockSpec(memory_space=pl.ANY)
    smem = pl.BlockSpec(memory_space=pltpu.SMEM)
    vmem = pl.BlockSpec(memory_space=pltpu.VMEM)
    return pl.pallas_call(
        kernel,
        name="diloco_step",
        out_shape=(
            jax.ShapeDtypeStruct((1, FEAT, COLS), BF16),
            jax.ShapeDtypeStruct((FEAT, COLS), F32),
        ),
        in_specs=[any_space] * 7 + [smem] * 3,
        out_specs=(vmem, vmem),
        scratch_shapes=[
            pltpu.VMEM((FEAT, COLS), BF16),
            pltpu.VMEM((2, FEAT, HALF), BF16),
            pltpu.VMEM((2, TOK, 2 * FEAT), BF16),
            pltpu.VMEM((2 * FEAT, 2 * TOK), BF16),
            pltpu.VMEM((TOK, COLS), BF16),
            pltpu.VMEM((FEAT, HD), jnp.int32),
            pltpu.VMEM((FEAT, HALF), BF16),
            pltpu.VMEM((NY - 1, YROWS, HALF), BF16),
            pltpu.VMEM((YROWS, HALF), F32),
            pltpu.VMEM((NZ - 1, ZROWS, HALF), F32),
            pltpu.VMEM((ZROWS, HALF), F32),
            pltpu.VMEM((ZROWS, HALF), F32),
            pltpu.VMEM((FEAT, HALF), F32),
            pltpu.VMEM((2, TOK, HALF), F32),
            pltpu.VMEM((2, TOK, HALF), F32),
            pltpu.VMEM((2, 2, TOK, HALF), BF16),
            pltpu.VMEM((2, PARTS, PROWS, HALF), BF16),
            pltpu.VMEM((2, PARTS, PROWS, HALF), BF16),
            pltpu.VMEM((2, PARTS, PROWS, HALF), F32),
            pltpu.VMEM((FEAT, COLS), BF16),
            pltpu.VMEM((FEAT, COLS), BF16),
            pltpu.VMEM((FEAT, COLS), BF16),
            pltpu.VMEM((FEAT, COLS), F32),
            pltpu.VMEM((FEAT, COLS), F32),
            pltpu.VMEM((8, HD), F32),
            pltpu.VMEM((4, 8, HD), F32),
            dma((8,)),
            dma((2,)),
            dma((2,)),
            dma((2,)),
            dma((2,)),
            dma((NY - 1,)),
            dma((NY - 1,)),
            dma((NZ - 1,)),
            dma((NZ - 1,)),
            dma,
            dma,
            dma((NZ - 1,)),
            dma((NZ - 1,)),
            dma((NY - 1,)),
            dma((NY - 1,)),
            dma((2,)),
            dma((2,)),
            dma((2,)),
            dma((2,)),
            dma((2, PARTS)),
            dma((2, PARTS)),
            dma((3,)),
            dma((3,)),
        ],
        compiler_params=pltpu.CompilerParams(
            collective_id=0, has_side_effects=True, vmem_limit_bytes=40 * 2**20
        ),
    )(*args)


def solution(mesh):
    placed = (
        P("rep", "fsdp", None),
        P("rep", "fsdp", None),
        P("rep", "fsdp", None),
        P("fsdp", None),
        P("fsdp", None),
        P("rep", "fsdp", None),
        P("rep", "fsdp", None),
        P("fsdp"),
        P(),
        P("rep"),
    )
    return jax.shard_map(
        local,
        mesh=mesh,
        in_specs=placed,
        out_specs=(P("rep", "fsdp", None), P("fsdp", None)),
        check_vma=False,
    )
```

time: 773 us -> 90.5 us (0.12)
  the two profiles are of different devices: /device:TPU:4 before, /device:TPU:1 now
where the time goes in v1:
time: 90.5 us; the launch traced here: 90.1 us
  Pallas kernels  75.8 us (84%)
  local copies, waits for them, and re-layouts  13 us (14%)
  between operations  1.31 us (1%)
    pallas_call x1, Pallas kernels, local(): pl.pallas_call(kernel, name='diloco_step', out_shape=(jax.ShapeDtypeStruc...  75.8 us
    unnamed x20, local copies, waits for them, and re-layouts  13 us

profile of v1, /device:TPU:1, one launch (start us, length us, event | category | flops | bytes accessed | tf_op | source)
XLA Modules:
  0.0 90.1 jit_solution(5364555408152848415)
XLA Ops:
  1.3 0.0 copy-start
  1.3 1.9 %copy-done = bf16[1,384,4096]{2,1,0:T(8,128)(2,1)S(1)} copy-done((bf16[1,384,4096]{2,1,0:T(8,128)(2,1)S(1)}, bf16[1,384,4096]{2,1,0:T(8,128)(2,1)}, u32[]{:S(2)}) %copy-start) | copy-done | bytes 3145752
  3.2 0.0 copy-start.1
  3.2 1.6 %copy-done.1 = f32[1024,512]{1,0:T(8,128)S(1)} copy-done((f32[1024,512]{1,0:T(8,128)S(1)}, f32[1024,512]{1,0:T(8,128)}, u32[]{:S(2)}) %copy-start.1) | copy-done | bytes 2097176
  4.8 0.0 copy-start.2
  4.8 1.2 %copy-done.2 = bf16[1,1024,512]{2,1,0:T(8,128)(2,1)S(1)} copy-done((bf16[1,1024,512]{2,1,0:T(8,128)(2,1)S(1)}, bf16[1,1024,512]{2,1,0:T(8,128)(2,1)}, u32[]{:S(2)}) %copy-start.2) | copy-done | bytes 1048600
  6.0 0.0 copy-start.3
  6.0 1.2 %copy-done.3 = bf16[1,1024,512]{2,1,0:T(8,128)(2,1)S(1)} copy-done((bf16[1,1024,512]{2,1,0:T(8,128)(2,1)S(1)}, bf16[1,1024,512]{2,1,0:T(8,128)(2,1)}, u32[]{:S(2)}) %copy-start.3) | copy-done | bytes 1048600
  7.2 0.0 copy-start.4
  7.2 1.2 %copy-done.4 = bf16[1,1024,512]{2,1,0:T(8,128)(2,1)S(1)} copy-done((bf16[1,1024,512]{2,1,0:T(8,128)(2,1)S(1)}, bf16[1,1024,512]{2,1,0:T(8,128)(2,1)}, u32[]{:S(2)}) %copy-start.4) | copy-done | bytes 1048600
  8.4 0.0 copy-start.5
  8.4 1.2 %copy-done.5 = bf16[1024,512]{1,0:T(8,128)(2,1)S(1)} copy-done((bf16[1024,512]{1,0:T(8,128)(2,1)S(1)}, bf16[1024,512]{1,0:T(8,128)(2,1)}, u32[]{:S(2)}) %copy-start.5) | copy-done | bytes 1048600
  9.7 0.0 copy-start.6
  9.7 1.0 %copy-done.6 = bf16[1,384,512]{2,1,0:T(8,128)(2,1)S(1)} copy-done((bf16[1,384,512]{2,1,0:T(8,128)(2,1)S(1)}, bf16[1,384,512]{2,1,0:T(8,128)(2,1)}, u32[]{:S(2)}) %copy-start.6) | copy-done | bytes 393240
  10.7 0.0 copy-start.7
  10.7 0.7 copy-done.7
  11.3 0.0 copy-start.8
  11.3 0.7 copy-done.8
  12.0 75.8 %diloco_step.1 = (bf16[1,1024,512]{2,1,0:T(8,128)(2,1)S(1)}, f32[1024,512]{1,0:T(8,128)S(1)}) custom-call(bf16[1,1024,512]{2,1,0:T(8,128)(2,1)S(1)} %copy-done.2, bf16[1,1024,512]{2,1,0:T(8,128)(2,1)S(1)} %copy-done.3, bf16[1,1024,512]{2,1,0:T(8,128)(2,1)S(1)} %copy-done.4, bf16[1024,512]{1,0:T(8,128)(2,1)S(1)} %copy-done.5, f32[1024,512]{1,0:T(8,128)S(1)} %copy-done.1, ...), custom_call_target="tpu_custom_call" | custom-call | tf_op jit(solution)/shard_map/diloco_step/pallas_call | solution.py:443
  87.8 1.0 %copy.15 = bf16[1,1024,512]{2,1,0:T(8,128)(2,1)} copy(bf16[1,1024,512]{2,1,0:T(8,128)(2,1)S(1)} %get-tuple-element.4) | data formatting | bytes 2097152
  88.8 1.3 %copy.16 = f32[1024,512]{1,0:T(8,128)} copy(f32[1024,512]{1,0:T(8,128)S(1)} %get-tuple-element.5) | data formatting | bytes 4194304
Async XLA Ops:
  1.3 1.9 %copy-start = (bf16[1,384,4096]{2,1,0:T(8,128)(2,1)S(1)}, bf16[1,384,4096]{2,1,0:T(8,128)(2,1)}, u32[]{:S(2)}) copy-start(bf16[1,384,4096]{2,1,0:T(8,128)(2,1)} %tokens.1) | copy-start | bytes 9437188
  3.2 1.6 %copy-start.1 = (f32[1024,512]{1,0:T(8,128)S(1)}, f32[1024,512]{1,0:T(8,128)}, u32[]{:S(2)}) copy-start(f32[1024,512]{1,0:T(8,128)} %momentum.1) | copy-start | bytes 6291460
  4.8 1.2 %copy-start.2 = (bf16[1,1024,512]{2,1,0:T(8,128)(2,1)S(1)}, bf16[1,1024,512]{2,1,0:T(8,128)(2,1)}, u32[]{:S(2)}) copy-start(bf16[1,1024,512]{2,1,0:T(8,128)(2,1)} %weight.1) | copy-start | bytes 3145732
  6.0 1.2 %copy-start.3 = (bf16[1,1024,512]{2,1,0:T(8,128)(2,1)S(1)}, bf16[1,1024,512]{2,1,0:T(8,128)(2,1)}, u32[]{:S(2)}) copy-start(bf16[1,1024,512]{2,1,0:T(8,128)(2,1)} %adam_first.1) | copy-start | bytes 3145732
  7.2 1.2 %copy-start.4 = (bf16[1,1024,512]{2,1,0:T(8,128)(2,1)S(1)}, bf16[1,1024,512]{2,1,0:T(8,128)(2,1)}, u32[]{:S(2)}) copy-start(bf16[1,1024,512]{2,1,0:T(8,128)(2,1)} %adam_second.1) | copy-start | bytes 3145732
  8.4 1.2 %copy-start.5 = (bf16[1024,512]{1,0:T(8,128)(2,1)S(1)}, bf16[1024,512]{1,0:T(8,128)(2,1)}, u32[]{:S(2)}) copy-start(bf16[1024,512]{1,0:T(8,128)(2,1)} %anchor.1) | copy-start | bytes 3145732
  9.7 1.0 %copy-start.6 = (bf16[1,384,512]{2,1,0:T(8,128)(2,1)S(1)}, bf16[1,384,512]{2,1,0:T(8,128)(2,1)}, u32[]{:S(2)}) copy-start(bf16[1,384,512]{2,1,0:T(8,128)(2,1)} %cotangent.1) | copy-start | bytes 1179652
  10.7 0.7 copy-start.7
  11.3 0.7 copy-start.8

commit v2 on v1

--- a/solution.py
+++ b/solution.py
@@ -34,6 +34,7 @@
 PROWS = FEAT // PARTS
 YROWS = FEAT // NY
 ZROWS = YROWS // NZ
+NEAR = (1, 7, 2, 6, 3, 5, 4)
 
 
 def place(x_lo, z, y, f):
@@ -48,15 +49,18 @@
     momentum,
     tokens,
     cotangent,
-    plan,
-    mix_weights,
+    plan_in,
+    mix_weights_in,
     mix_index,
     new_weight,
     new_momentum,
+    plan,
+    mix_weights,
     wown,
     wrecv,
     tch,
     tt,
+    begun,
     cot,
     mask,
     picked,
@@ -79,6 +83,7 @@
     level,
     factor,
     sq,
+    small_sem,
     load_sem,
     wsend_sem,
     wrecv_sem,
@@ -126,6 +131,12 @@
     def columns(index):
         return pl.ds(pl.multiple_of(index * FEAT, FEAT), FEAT)
 
+    small = [
+        pltpu.make_async_copy(plan_in, plan, small_sem.at[0]),
+        pltpu.make_async_copy(mix_weights_in, mix_weights, small_sem.at[1]),
+    ]
+    for copy in small:
+        copy.start()
     loads = [
         pltpu.make_async_copy(weight.at[0], wown, load_sem.at[0]),
         pltpu.make_async_copy(
@@ -142,6 +153,9 @@
     ]
     for copy in loads:
         copy.start()
+
+    for copy in small:
+        copy.wait()
 
     def mark(i, _):
         mask[pl.ds(pl.multiple_of(i * ROWS, ROWS), ROWS), :] = jnp.full((ROWS, HD), plan[i], jnp.int32)
@@ -257,11 +271,55 @@
     d_copies = []
     g_copies = []
 
-    def project(t, j):
-        mine = jnp.dot(
+    def prepare(t, j):
+        begun[t, j] = jnp.dot(
             tch[t, :, own_block], wown[:, j * HALF : (j + 1) * HALF], preferred_element_type=F32
         )
-        return mine + jnp.dot(tch[t, :, across_block], wrecv[j], preferred_element_type=F32)
+
+    def project(t, j):
+        return begun[t, j] + jnp.dot(tch[t, :, across_block], wrecv[j], preferred_element_type=F32)
+
+    def add_z():
+        for copy in z_copies:
+            copy.wait_recv()
+        total = ysum[pl.ds(pl.multiple_of(z * ZROWS, ZROWS), ZROWS), :]
+        for d in range(NZ - 1):
+            total = total + zrecv[d]
+        zsum[...] = total
+        x_copy.start()
+
+    def slice_of(d):
+        start = y * YROWS + ((z + NZ - d) % NZ) * ZROWS
+        return pl.ds(pl.multiple_of(start, ZROWS), ZROWS)
+
+    def spread(d):
+        rows = slice_of(d)
+        for e in range(NY - 1):
+            copy = remote(
+                mean.at[rows], mean.at[rows], aysend_sem.at[d, e], ayrecv_sem.at[d, e], y_peers[e]
+            )
+            copy.start()
+            ay_copies.append(copy)
+
+    def add_x():
+        x_copy.wait_recv()
+        rows = slice_of(0)
+        mean[rows, :] = (zsum[...] + xrecv[...]) * (1.0 / REPS)
+        for d in NEAR:
+            az_copies[d] = remote(
+                mean.at[rows], mean.at[rows], azsend_sem.at[d - 1], azrecv_sem.at[d - 1], z_peers[d - 1]
+            )
+            az_copies[d].start()
+        spread(0)
+
+    def forward(*steps):
+        for d in steps:
+            az_copies[d].wait_recv()
+            spread(d)
+
+    x_copy = remote(zsum, xrecv, xsend_sem, xrecv_sem, x_peer)
+    az_copies = {}
+    ay_copies = []
 
     def chunk(j):
         w_copies[j].wait_recv()
@@ -283,6 +341,8 @@
         d_copy = remote(dch.at[j, 0], dch.at[j, 1], dsend_sem.at[j], drecv_sem.at[j], mate)
         d_copy.start()
         d_copies.append(d_copy)
+        if j == 0:
+            add_z()
         d_copy.wait_recv()
 
         def grad(at):
@@ -302,45 +362,14 @@
         for i in range(PARTS):
             gown[j, i] = grad(i * PROWS)
 
+    for t in range(2):
+        for j in range(2):
+            prepare(t, j)
+
     chunk(0)
-
-    for copy in z_copies:
-        copy.wait_recv()
-    total = ysum[pl.ds(pl.multiple_of(z * ZROWS, ZROWS), ZROWS), :]
-    for d in range(NZ - 1):
-        total = total + zrecv[d]
-    zsum[...] = total
-    x_copy = remote(zsum, xrecv, xsend_sem, xrecv_sem, x_peer)
-    x_copy.start()
-    x_copy.wait_recv()
-    mine = pl.ds(pl.multiple_of(y * YROWS + z * ZROWS, ZROWS), ZROWS)
-    mean[mine, :] = (zsum[...] + xrecv[...]) * (1.0 / REPS)
-    az_copies = []
-    for d in range(1, NZ):
-        az_copies.append(
-            remote(
-                mean.at[mine], mean.at[mine], azsend_sem.at[d - 1], azrecv_sem.at[d - 1], z_peers[d - 1]
-            )
-        )
-        az_copies[-1].start()
-
+    add_x()
     chunk(1)
-
-    for copy in az_copies:
-        copy.wait_recv()
-    block = pl.ds(pl.multiple_of(y * YROWS, YROWS), YROWS)
-    ay_copies = []
-    for d in range(1, NY):
-        ay_copies.append(
-            remote(
-                mean.at[block],
-                mean.at[block],
-                aysend_sem.at[d - 1],
-                ayrecv_sem.at[d - 1],
-                y_peers[d - 1],
-            )
-        )
-        ay_copies[-1].start()
+    forward(*NEAR)
 
     def gather(j, i, total):
         g_copies[j * PARTS + i].wait_recv()
@@ -430,7 +459,7 @@
 
             lax.fori_loop(0, PROWS // 16, adam, 0, unroll=4)
 
-    sent = w_copies + t_copies + y_copies + z_copies + [x_copy] + az_copies + ay_copies
+    sent = w_copies + t_copies + y_copies + z_copies + [x_copy] + list(az_copies.values()) + ay_copies
     for copy in sent + p_copies + d_copies + g_copies + q_copies:
         copy.wait_send()
 
@@ -438,7 +467,6 @@
 def local(*args):
     dma = pltpu.SemaphoreType.DMA
     any_space = pl.BlockSpec(memory_space=pl.ANY)
-    smem = pl.BlockSpec(memory_space=pltpu.SMEM)
     vmem = pl.BlockSpec(memory_space=pltpu.VMEM)
     return pl.pallas_call(
         kernel,
@@ -447,13 +475,16 @@
             jax.ShapeDtypeStruct((1, FEAT, COLS), BF16),
             jax.ShapeDtypeStruct((FEAT, COLS), F32),
         ),
-        in_specs=[any_space] * 7 + [smem] * 3,
+        in_specs=[any_space] * 9 + [pl.BlockSpec(memory_space=pltpu.SMEM)],
         out_specs=(vmem, vmem),
         scratch_shapes=[
+            pltpu.SMEM((FEAT // ROWS,), jnp.int32),
+            pltpu.SMEM((4,), F32),
             pltpu.VMEM((FEAT, COLS), BF16),
             pltpu.VMEM((2, FEAT, HALF), BF16),
             pltpu.VMEM((2, TOK, 2 * FEAT), BF16),
             pltpu.VMEM((2 * FEAT, 2 * TOK), BF16),
+            pltpu.VMEM((2, 2, TOK, HALF), F32),
             pltpu.VMEM((TOK, COLS), BF16),
             pltpu.VMEM((FEAT, HD), jnp.int32),
             pltpu.VMEM((FEAT, HALF), BF16),
@@ -476,6 +507,7 @@
             pltpu.VMEM((FEAT, COLS), F32),
             pltpu.VMEM((8, HD), F32),
             pltpu.VMEM((4, 8, HD), F32),
+            dma((2,)),
             dma((8,)),
             dma((2,)),
             dma((2,)),
@@ -489,8 +521,8 @@
             dma,
             dma((NZ - 1,)),
             dma((NZ - 1,)),
-            dma((NY - 1,)),
-            dma((NY - 1,)),
+            dma((NZ, NY - 1)),
+            dma((NZ, NY - 1)),
             dma((2,)),
             dma((2,)),
             dma((2,)),
@@ -503,7 +535,7 @@
         compiler_params=pltpu.CompilerParams(
             collective_id=0, has_side_effects=True, vmem_limit_bytes=40 * 2**20
         ),
-    )(*args)
+    )(*[pltpu.with_memory_space_constraint(a, pltpu.HBM) for a in args[:9]], args[9])
 
 
 def solution(mesh):

time: 90.5 us -> 67.5 us (0.75)
  Pallas kernels: 75.8 us -> 63.8 us
  local copies, waits for them, and re-layouts: 13 us -> 2.29 us
    pallas_call x1, Pallas kernels: 75.8 us -> 63.8 us  [local(): pl.pallas_call(kernel, name='diloco_step', out_shape=(jax.ShapeDtypeStruc...]
    unnamed x20 -> x2, local copies, waits for them, and re-layouts: 13 us -> 2.29 us
where the time goes in v2:
time: 67.5 us; the launch traced here: 67.4 us
  Pallas kernels  63.8 us (95%)
  local copies, waits for them, and re-layouts  2.29 us (3%)
  between operations  1.29 us (2%)
    pallas_call x1, Pallas kernels, local(): pl.pallas_call(kernel, name='diloco_step', out_shape=(jax.ShapeDtypeStruc...  63.8 us
    unnamed x2, local copies, waits for them, and re-layouts  2.29 us

profile of v2, /device:TPU:1, one launch (start us, length us, event | category | flops | bytes accessed | tf_op | source)
XLA Modules:
  0.0 67.4 jit_solution(4148133168839671693)
XLA Ops:
  1.3 63.8 %diloco_step.1 = (bf16[1,1024,512]{2,1,0:T(8,128)(2,1)S(1)}, f32[1024,512]{1,0:T(8,128)S(1)}) custom-call(bf16[1,1024,512]{2,1,0:T(8,128)(2,1)} %weight.1, bf16[1,1024,512]{2,1,0:T(8,128)(2,1)} %adam_first.1, bf16[1,1024,512]{2,1,0:T(8,128)(2,1)} %adam_second.1, bf16[1024,512]{1,0:T(8,128)(2,1)} %anchor.1, f32[1024,512]{1,0:T(8,128)} %momentum.1, ...), custom_call_target="tpu_custom_call" | custom-call | tf_op jit(solution)/shard_map/diloco_step/pallas_call | solution.py:471
  65.1 1.0 %copy.15 = bf16[1,1024,512]{2,1,0:T(8,128)(2,1)} copy(bf16[1,1024,512]{2,1,0:T(8,128)(2,1)S(1)} %get-tuple-element.4) | data formatting | bytes 2097152
  66.1 1.3 %copy.16 = f32[1024,512]{1,0:T(8,128)} copy(f32[1024,512]{1,0:T(8,128)S(1)} %get-tuple-element.5) | data formatting | bytes 4194304

commit v3 on v2

--- a/solution.py
+++ b/solution.py
@@ -83,6 +83,7 @@
     level,
     factor,
     sq,
+    ready_sem,
     small_sem,
     load_sem,
     wsend_sem,
@@ -124,9 +125,14 @@
     x_peer = place(1 - x_lo, z, y, f)
 
     barrier = pltpu.get_barrier_semaphore()
-    peers = [across, mate, diag, x_peer] + y_peers + z_peers
+    peers = [across, mate, diag, x_peer] + y_peers
     for peer in peers:
         pl.semaphore_signal(barrier, inc=1, device_id=peer, device_id_type=MESH)
+    for d in range(1, NZ):
+
+        @pl.when((z + d) % NZ > z)
+        def _(peer=z_peers[d - 1]):
+            pl.semaphore_signal(barrier, inc=1, device_id=peer, device_id_type=MESH)
 
     def columns(index):
         return pl.ds(pl.multiple_of(index * FEAT, FEAT), FEAT)
@@ -154,16 +160,7 @@
     for copy in loads:
         copy.start()
 
-    for copy in small:
-        copy.wait()
-
-    def mark(i, _):
-        mask[pl.ds(pl.multiple_of(i * ROWS, ROWS), ROWS), :] = jnp.full((ROWS, HD), plan[i], jnp.int32)
-        return 0
-
-    lax.fori_loop(0, FEAT // ROWS, mark, 0, unroll=8)
-
-    pl.semaphore_wait(barrier, len(peers))
+    pl.semaphore_wait(barrier, len(peers) + z)
 
     def remote(src, dst, send, recv, to):
         return pltpu.make_async_remote_copy(
@@ -190,6 +187,21 @@
     ]
     for copy in t_copies:
         copy.start()
+    for d in range(1, NZ):
+
+        @pl.when((z + d) % NZ < z)
+        def _(peer=z_peers[d - 1]):
+            pl.semaphore_signal(ready_sem, inc=1, device_id=peer, device_id_type=MESH)
+
+
+    for copy in small:
+        copy.wait()
+
+    def mark(i, _):
+        mask[pl.ds(pl.multiple_of(i * ROWS, ROWS), ROWS), :] = jnp.full((ROWS, HD), plan[i], jnp.int32)
+        return 0
+
+    lax.fori_loop(0, FEAT // ROWS, mark, 0, unroll=8)
 
     loads[0].wait()
 
@@ -203,23 +215,23 @@
                 picked[rows, k * HD : (k + 1) * HD] = jnp.where(chosen, low, high).astype(BF16)
             return 0
 
-        lax.fori_loop(0, YROWS // 32, body, 0, unroll=2)
-
-    y_copies = []
-    for d in range(1, NY):
-        start = ((y + d) % NY) * YROWS
-        pick(start)
-        y_copies.append(
-            remote(
-                picked.at[pl.ds(pl.multiple_of(start, YROWS), YROWS)],
-                yrecv.at[d - 1],
-                ysend_sem.at[d - 1],
-                yrecv_sem.at[d - 1],
+        lax.fori_loop(0, YROWS // 64, body, 0, unroll=2)
+
+    y_copies = [[], []]
+    for part in range(2):
+        for d in range(1, NY):
+            start = ((y + d) % NY) * YROWS + part * (YROWS // 2)
+            pick(start)
+            copy = remote(
+                picked.at[pl.ds(pl.multiple_of(start, YROWS // 2), YROWS // 2)],
+                yrecv.at[d - 1, pl.ds(part * (YROWS // 2), YROWS // 2)],
+                ysend_sem.at[d - 1, part],
+                yrecv_sem.at[d - 1, part],
                 y_peers[d - 1],
             )
-        )
-        y_copies[-1].start()
-    pick(y * YROWS)
+            copy.start()
+            y_copies[part].append(copy)
+        pick(y * YROWS + part * (YROWS // 2))
 
     def turn(t):
         def body(i, _):
@@ -233,9 +245,9 @@
     loads[2].wait()
     turn(0)
 
-    for copy in y_copies:
+    for copy in t_copies:
         copy.wait_recv()
-
+    turn(1)
     def add_y(i, _):
         at = pl.multiple_of(i * 32, 32)
         rows = pl.ds(at, 32)
@@ -245,7 +257,6 @@
         ysum[rows, :] = total
         return 0
 
-    lax.fori_loop(0, YROWS // 32, add_y, 0)
     z_copies = []
     for d in range(1, NZ):
         start = pl.multiple_of(((z + d) % NZ) * ZROWS, ZROWS)
@@ -258,11 +269,19 @@
                 z_peers[d - 1],
             )
         )
-        z_copies[-1].start()
-
-    for copy in t_copies:
-        copy.wait_recv()
-    turn(1)
+    for part in range(2):
+        for copy in y_copies[part]:
+            copy.wait_recv()
+        lax.fori_loop(part * NZ // 2, (part + 1) * NZ // 2, add_y, 0)
+        if part == 0:
+
+            @pl.when(z < NZ - 1)
+            def _():
+                pl.semaphore_wait(ready_sem, NZ - 1 - z)
+
+        for d in range(1, NZ):
+            pl.when(((z + d) % NZ) // (NZ // 2) == part)(z_copies[d - 1].start)
+
     loads[3].wait()
 
     own_block = pl.ds(0, FEAT)
@@ -459,7 +478,7 @@
 
             lax.fori_loop(0, PROWS // 16, adam, 0, unroll=4)
 
-    sent = w_copies + t_copies + y_copies + z_copies + [x_copy] + list(az_copies.values()) + ay_copies
+    sent = w_copies + t_copies + y_copies[0] + y_copies[1] + z_copies + [x_copy] + list(az_copies.values()) + ay_copies
     for copy in sent + p_copies + d_copies + g_copies + q_copies:
         copy.wait_send()
 
@@ -507,14 +526,15 @@
             pltpu.VMEM((FEAT, COLS), F32),
             pltpu.VMEM((8, HD), F32),
             pltpu.VMEM((4, 8, HD), F32),
+            pltpu.SemaphoreType.REGULAR,
             dma((2,)),
             dma((8,)),
             dma((2,)),
             dma((2,)),
             dma((2,)),
             dma((2,)),
-            dma((NY - 1,)),
-            dma((NY - 1,)),
+            dma((NY - 1, 2)),
+            dma((NY - 1, 2)),
             dma((NZ - 1,)),
             dma((NZ - 1,)),
             dma,

time: 67.5 us -> 63.6 us (0.942)
  Pallas kernels: 63.8 us -> 59.9 us
    pallas_call x1, Pallas kernels: 63.8 us -> 59.9 us  [local(): pl.pallas_call(kernel, name='diloco_step', out_shape=(jax.ShapeDtypeStruc...]
where the time goes in v3:
time: 63.6 us; the launch traced here: 63.5 us
  Pallas kernels  59.9 us (94%)
  local copies, waits for them, and re-layouts  2.29 us (4%)
  between operations  1.29 us (2%)
    pallas_call x1, Pallas kernels, local(): pl.pallas_call(kernel, name='diloco_step', out_shape=(jax.ShapeDtypeStruc...  59.9 us
    unnamed x2, local copies, waits for them, and re-layouts  2.29 us

profile of v3, /device:TPU:1, one launch (start us, length us, event | category | flops | bytes accessed | tf_op | source)
XLA Modules:
  0.0 63.5 jit_solution(2483767305301697160)
XLA Ops:
  1.3 59.9 %diloco_step.1 = (bf16[1,1024,512]{2,1,0:T(8,128)(2,1)S(1)}, f32[1024,512]{1,0:T(8,128)S(1)}) custom-call(bf16[1,1024,512]{2,1,0:T(8,128)(2,1)} %weight.1, bf16[1,1024,512]{2,1,0:T(8,128)(2,1)} %adam_first.1, bf16[1,1024,512]{2,1,0:T(8,128)(2,1)} %adam_second.1, bf16[1024,512]{1,0:T(8,128)(2,1)} %anchor.1, f32[1024,512]{1,0:T(8,128)} %momentum.1, ...), custom_call_target="tpu_custom_call" | custom-call | tf_op jit(solution)/shard_map/diloco_step/pallas_call | solution.py:490
  61.2 1.0 %copy.15 = bf16[1,1024,512]{2,1,0:T(8,128)(2,1)} copy(bf16[1,1024,512]{2,1,0:T(8,128)(2,1)S(1)} %get-tuple-element.4) | data formatting | bytes 2097152
  62.2 1.3 %copy.16 = f32[1024,512]{1,0:T(8,128)} copy(f32[1024,512]{1,0:T(8,128)S(1)} %get-tuple-element.5) | data formatting | bytes 4194304

commit v4 on v3

--- a/solution.py
+++ b/solution.py
@@ -52,8 +52,14 @@
     plan_in,
     mix_weights_in,
     mix_index,
-    new_weight,
-    new_momentum,
+    linear,
+    square,
+    total_squares,
+    level,
+    moved_out,
+    rate,
+    kept_first,
+    kept_second,
     plan,
     mix_weights,
     wown,
@@ -80,8 +86,6 @@
     second,
     base,
     old,
-    level,
-    factor,
     sq,
     ready_sem,
     small_sem,
@@ -396,11 +400,12 @@
         def body(s, total):
             rows = pl.ds(pl.multiple_of(s * 32, 32), 32)
             grad = (gown[j, i, rows, :] + grecv[j, i, rows, :].astype(F32)) * (1.0 / (4 * TOK))
-            gown[j, i, rows, :] = grad
-            square = grad * grad
+            linear[j, i, rows, :] = (1.0 - BETA_ONE) * grad
+            power = grad * grad
+            square[j, i, rows, :] = (1.0 - BETA_TWO) * power
             for r in range(4):
                 for k in range(HALF // HD):
-                    total = total + square[r * 8 : (r + 1) * 8, k * HD : (k + 1) * HD]
+                    total = total + power[r * 8 : (r + 1) * 8, k * HD : (k + 1) * HD]
             return total
 
         return lax.fori_loop(0, PROWS // 32, body, total, unroll=2)
@@ -411,6 +416,14 @@
 
     for copy in loads[4:]:
         copy.wait()
+
+    def decay(i, _):
+        rows = pl.ds(pl.multiple_of(i * 16, 16), 16)
+        kept_first[rows, :] = BETA_ONE * first[rows, :].astype(F32)
+        kept_second[rows, :] = BETA_TWO * second[rows, :].astype(F32)
+        return 0
+
+    lax.fori_loop(0, FEAT // 16, decay, 0)
     choice = mix_index[0]
     alpha = mix_weights[0]
     for k in range(1, 4):
@@ -421,6 +434,8 @@
     def outer_step(i, _):
         rows = pl.ds(pl.multiple_of(i * 16, 16), 16)
         row_frag = mask[rows, :]
+        for index in range(2):
+            rate[index, rows, :] = jnp.where(row_frag == index, alpha * LEARN_RATE, LEARN_RATE)
         for k in range(HALF // HD):
             middle = mean[rows, k * HD : (k + 1) * HD]
             for index in range(2):
@@ -432,7 +447,7 @@
                 average = start - middle
                 moved = MOMENT_COEF * before + average
                 outer = start - OUTER_RATE * (average + MOMENT_COEF * moved)
-                new_momentum[rows, at : at + HD] = jnp.where(chosen, moved, before)
+                moved_out[rows, at : at + HD] = jnp.where(chosen, moved, before)
                 level[rows, at : at + HD] = jnp.where(
                     chosen, alpha * wide + (1.0 - alpha) * outer, wide
                 )
@@ -449,53 +464,80 @@
         q_copies[-1].start()
     for copy in q_copies:
         copy.wait_recv()
-    everything = jnp.sum(sq[0] + sq[1] + sq[2] + sq[3], keepdims=True)
-    clip = jnp.minimum(1.0, CLIP / jnp.sqrt(everything + 1e-12))
-    factor[...] = jnp.broadcast_to(clip, (8, HD))
-
-    for j in range(2):
-        for i in range(PARTS):
-
-            def adam(s, _, j=j, i=i):
-                at = pl.multiple_of(s * 16, 16)
-                rows = pl.ds(pl.multiple_of(i * PROWS + s * 16, 16), 16)
-                ratio = jnp.concatenate([factor[...]] * 2, axis=0)
-                chosen_row = mask[rows, :]
-                rate = jnp.where(chosen_row == j, alpha * LEARN_RATE, LEARN_RATE)
-                for k in range(HALF // HD):
-                    c = j * HALF + k * HD
-                    clipped = gown[j, i, pl.ds(at, 16), k * HD : (k + 1) * HD] * ratio
-                    one = BETA_ONE * first[rows, c : c + HD].astype(F32) + (1.0 - BETA_ONE) * clipped
-                    two = (
-                        BETA_TWO * second[rows, c : c + HD].astype(F32)
-                        + (1.0 - BETA_TWO) * clipped * clipped
-                    )
-                    step = one / (jnp.sqrt(two) + ADAM_EPS)
-                    new_weight[0, rows, c : c + HD] = (
-                        level[rows, c : c + HD] - rate * step
-                    ).astype(BF16)
-                return 0
-
-            lax.fori_loop(0, PROWS // 16, adam, 0, unroll=4)
+    total_squares[...] = sq[0] + sq[1] + sq[2] + sq[3]
 
     sent = w_copies + t_copies + y_copies[0] + y_copies[1] + z_copies + [x_copy] + list(az_copies.values()) + ay_copies
     for copy in sent + p_copies + d_copies + g_copies + q_copies:
         copy.wait_send()
+
+
+def update(
+    linear,
+    square,
+    total_squares,
+    level,
+    moved,
+    rate,
+    kept_first,
+    kept_second,
+    new_weight,
+    new_momentum,
+    result,
+    weight_sem,
+    momentum_sem,
+):
+    momentum_copy = pltpu.make_async_copy(moved, new_momentum, momentum_sem)
+    momentum_copy.start()
+    everything = jnp.sum(total_squares[...], keepdims=True)
+    clip = jnp.minimum(1.0, CLIP / jnp.sqrt(everything + 1e-12))
+    ratio = jnp.broadcast_to(clip, (16, HD))
+    ratio_squared = ratio * ratio
+    copies = []
+    for i in range(PARTS):
+
+        def adam(s, _, i=i):
+            at = pl.multiple_of(s * 16, 16)
+            rows = pl.ds(pl.multiple_of(i * PROWS + s * 16, 16), 16)
+            for j in range(2):
+                speed = rate[j, rows, :]
+                for k in range(HALF // HD):
+                    c = j * HALF + k * HD
+                    block = (j, i, pl.ds(at, 16), slice(k * HD, (k + 1) * HD))
+                    one = kept_first[rows, c : c + HD] + linear[block] * ratio
+                    two = kept_second[rows, c : c + HD] + square[block] * ratio_squared
+                    step = one / (two * lax.rsqrt(two) + ADAM_EPS)
+                    result[rows, c : c + HD] = (level[rows, c : c + HD] - speed * step).astype(BF16)
+            return 0
+
+        lax.fori_loop(0, PROWS // 16, adam, 0, unroll=4)
+        block = pl.ds(i * PROWS, PROWS)
+        copy = pltpu.make_async_copy(result.at[block], new_weight.at[0, block], weight_sem.at[i])
+        copy.start()
+        copies.append(copy)
+    for copy in copies:
+        copy.wait()
+    momentum_copy.wait()
 
 
 def local(*args):
     dma = pltpu.SemaphoreType.DMA
     any_space = pl.BlockSpec(memory_space=pl.ANY)
     vmem = pl.BlockSpec(memory_space=pltpu.VMEM)
-    return pl.pallas_call(
+    parts = pl.pallas_call(
         kernel,
         name="diloco_step",
         out_shape=(
-            jax.ShapeDtypeStruct((1, FEAT, COLS), BF16),
+            jax.ShapeDtypeStruct((2, PARTS, PROWS, HALF), F32),
+            jax.ShapeDtypeStruct((2, PARTS, PROWS, HALF), F32),
+            jax.ShapeDtypeStruct((8, HD), F32),
+            jax.ShapeDtypeStruct((FEAT, COLS), F32),
+            jax.ShapeDtypeStruct((FEAT, COLS), F32),
+            jax.ShapeDtypeStruct((2, FEAT, HD), F32),
+            jax.ShapeDtypeStruct((FEAT, COLS), F32),
             jax.ShapeDtypeStruct((FEAT, COLS), F32),
         ),
         in_specs=[any_space] * 9 + [pl.BlockSpec(memory_space=pltpu.SMEM)],
-        out_specs=(vmem, vmem),
+        out_specs=(vmem,) * 8,
         scratch_shapes=[
             pltpu.SMEM((FEAT // ROWS,), jnp.int32),
             pltpu.SMEM((4,), F32),
@@ -523,8 +565,6 @@
             pltpu.VMEM((FEAT, COLS), BF16),
             pltpu.VMEM((FEAT, COLS), BF16),
             pltpu.VMEM((FEAT, COLS), F32),
-            pltpu.VMEM((FEAT, COLS), F32),
-            pltpu.VMEM((8, HD), F32),
             pltpu.VMEM((4, 8, HD), F32),
             pltpu.SemaphoreType.REGULAR,
             dma((2,)),
@@ -556,6 +596,18 @@
             collective_id=0, has_side_effects=True, vmem_limit_bytes=40 * 2**20
         ),
     )(*[pltpu.with_memory_space_constraint(a, pltpu.HBM) for a in args[:9]], args[9])
+    return pl.pallas_call(
+        update,
+        name="adam_blend",
+        out_shape=(
+            jax.ShapeDtypeStruct((1, FEAT, COLS), BF16),
+            jax.ShapeDtypeStruct((FEAT, COLS), F32),
+        ),
+        in_specs=[vmem] * 8,
+        out_specs=(any_space, any_space),
+        scratch_shapes=[pltpu.VMEM((FEAT, COLS), BF16), dma((PARTS,)), dma],
+        compiler_params=pltpu.CompilerParams(vmem_limit_bytes=16 * 2**20),
+    )(*parts)
 
 
 def solution(mesh):

time: 63.6 us -> 61.2 us (0.962)
  local copies, waits for them, and re-layouts: 2.29 us -> 0 us
    unnamed x2 -> x0, local copies, waits for them, and re-layouts: 2.29 us -> none
    pallas_call x1, Pallas kernels: 59.9 us -> 57.8 us  [local(): pl.pallas_call(kernel, name='diloco_step', out_shape=(jax.ShapeDtypeStruc...]
    pallas_call x0 -> x1, Pallas kernels: none -> 2.08 us  [local(): pl.pallas_call(update, name='adam_blend', out_shape=(jax.ShapeDtypeStruct...]
where the time goes in v4:
time: 61.2 us; the launch traced here: 61.1 us
  Pallas kernels  59.8 us (98%)
  between operations  1.29 us (2%)
    pallas_call x1, Pallas kernels, local(): pl.pallas_call(kernel, name='diloco_step', out_shape=(jax.ShapeDtypeStruc...  57.8 us
    pallas_call x1, Pallas kernels, local(): pl.pallas_call(update, name='adam_blend', out_shape=(jax.ShapeDtypeStruct...  2.08 us

profile of v4, /device:TPU:1, one launch (start us, length us, event | category | flops | bytes accessed | tf_op | source)
XLA Modules:
  0.0 61.1 jit_solution(7278581824809269132)
XLA Ops:
  1.3 57.8 %diloco_step.1 = (f32[2,4,256,256]{3,2,1,0:T(8,128)S(1)}, f32[2,4,256,256]{3,2,1,0:T(8,128)S(1)}, f32[8,128]{1,0:T(8,128)S(1)}, f32[1024,512]{1,0:T(8,128)S(1)},...) custom-call(bf16[1,1024,512]{2,1,0:T(8,128)(2,1)} %weight.1, ...), custom_call_target="tpu_custom_call" | custom-call | tf_op jit(solution)/shard_map/diloco_step/pallas_call | solution.py:526
  59.0 2.1 %adam_blend.1 = (bf16[1,1024,512]{2,1,0:T(8,128)(2,1)}, f32[1024,512]{1,0:T(8,128)}) custom-call(f32[2,4,256,256]{3,2,1,0:T(8,128)S(1)} %get-tuple-element.10.linear, f32[2,4,256,256]{3,2,1,0:T(8,128)S(1)} %get-tuple-element.11.square, f32[8,128]{1,0:T(8,128)S(1)} %get-tuple-element.12.total_squares, f32[1024,512]{1,0:T(8,128)S(1)} %get-tuple-element.13.level, ...), custom_call_target="tpu_custom_call" | custom-call | tf_op jit(solution)/shard_map/adam_blend/pallas_call | solution.py:599

commit v5 on v4

--- a/solution.py
+++ b/solution.py
@@ -118,7 +118,8 @@
     x_lo = rep // (NZ * NY)
     z = (rep // NY) % NZ
     y = rep % NY
-    mate_f = f + 1 - 2 * (f % 2)
+    core = f % 2
+    mate_f = f + 1 - 2 * core
     across_f = (f + 2) % 4
     diag_f = 3 - f
     mate = (rep, mate_f)
@@ -129,18 +130,48 @@
     x_peer = place(1 - x_lo, z, y, f)
 
     barrier = pltpu.get_barrier_semaphore()
-    peers = [across, mate, diag, x_peer] + y_peers
-    for peer in peers:
-        pl.semaphore_signal(barrier, inc=1, device_id=peer, device_id_type=MESH)
+    pl.semaphore_signal(barrier, inc=1, device_id=across, device_id_type=MESH)
+
+    @pl.when(core == 1)
+    def _():
+        for peer in (mate, diag):
+            pl.semaphore_signal(barrier, inc=1, device_id=peer, device_id_type=MESH)
+
+    for d in range(1, NY):
+
+        @pl.when((y + d) % NY > y)
+        def _(peer=y_peers[d - 1]):
+            pl.semaphore_signal(barrier, inc=1, device_id=peer, device_id_type=MESH)
+
     for d in range(1, NZ):
 
         @pl.when((z + d) % NZ > z)
         def _(peer=z_peers[d - 1]):
             pl.semaphore_signal(barrier, inc=1, device_id=peer, device_id_type=MESH)
 
+    @pl.when(x_lo == 0)
+    def _():
+        pl.semaphore_signal(barrier, inc=1, device_id=x_peer, device_id_type=MESH)
+
+
     def columns(index):
         return pl.ds(pl.multiple_of(index * FEAT, FEAT), FEAT)
 
+    pl.semaphore_wait(barrier, 3 - 2 * core + x_lo + y + z)
+
+    def remote(src, dst, send, recv, to):
+        return pltpu.make_async_remote_copy(
+            src_ref=src, dst_ref=dst, send_sem=send, recv_sem=recv, device_id=to, device_id_type=MESH
+        )
+
+    w_copies = [
+        remote(
+            weight.at[0, :, pl.ds(j * HALF, HALF)], wrecv.at[j], wsend_sem.at[j], wrecv_sem.at[j], across
+        )
+        for j in range(2)
+    ]
+    for copy in w_copies:
+        copy.start()
     small = [
         pltpu.make_async_copy(plan_in, plan, small_sem.at[0]),
         pltpu.make_async_copy(mix_weights_in, mix_weights, small_sem.at[1]),
@@ -164,21 +195,6 @@
     for copy in loads:
         copy.start()
 
-    pl.semaphore_wait(barrier, len(peers) + z)
-
-    def remote(src, dst, send, recv, to):
-        return pltpu.make_async_remote_copy(
-            src_ref=src, dst_ref=dst, send_sem=send, recv_sem=recv, device_id=to, device_id_type=MESH
-        )
-
-    w_copies = [
-        remote(
-            weight.at[0, :, pl.ds(j * HALF, HALF)], wrecv.at[j], wsend_sem.at[j], wrecv_sem.at[j], across
-        )
-        for j in range(2)
-    ]
-    for copy in w_copies:
-        copy.start()
     t_copies = [
         remote(
             tokens.at[0, :, columns(index)],
@@ -189,13 +205,26 @@
         )
         for b, index in enumerate((mate_f, diag_f))
     ]
-    for copy in t_copies:
-        copy.start()
+    @pl.when(core == 0)
+    def _():
+        for peer in (mate, diag):
+            pl.semaphore_signal(ready_sem.at[2], inc=1, device_id=peer, device_id_type=MESH)
+
     for d in range(1, NZ):
 
         @pl.when((z + d) % NZ < z)
         def _(peer=z_peers[d - 1]):
-            pl.semaphore_signal(ready_sem, inc=1, device_id=peer, device_id_type=MESH)
+            pl.semaphore_signal(ready_sem.at[1], inc=1, device_id=peer, device_id_type=MESH)
+
+    @pl.when(x_lo == 1)
+    def _():
+        pl.semaphore_signal(ready_sem.at[1], inc=1, device_id=x_peer, device_id_type=MESH)
+
+    for d in range(1, NY):
+
+        @pl.when((y + d) % NY < y)
+        def _(peer=y_peers[d - 1]):
+            pl.semaphore_signal(ready_sem.at[0], inc=1, device_id=peer, device_id_type=MESH)
 
 
     for copy in small:
@@ -226,6 +255,12 @@
         for d in range(1, NY):
             start = ((y + d) % NY) * YROWS + part * (YROWS // 2)
             pick(start)
+            if part == 0 and d == 1:
+
+                @pl.when(y < NY - 1)
+                def _():
+                    pl.semaphore_wait(ready_sem.at[0], NY - 1 - y)
+
             copy = remote(
                 picked.at[pl.ds(pl.multiple_of(start, YROWS // 2), YROWS // 2)],
                 yrecv.at[d - 1, pl.ds(part * (YROWS // 2), YROWS // 2)],
@@ -236,6 +271,13 @@
             copy.start()
             y_copies[part].append(copy)
         pick(y * YROWS + part * (YROWS // 2))
+
+    @pl.when(core == 1)
+    def _():
+        pl.semaphore_wait(ready_sem.at[2], 2)
+
+    for copy in t_copies:
+        copy.start()
 
     def turn(t):
         def body(i, _):
@@ -279,9 +321,9 @@
         lax.fori_loop(part * NZ // 2, (part + 1) * NZ // 2, add_y, 0)
         if part == 0:
 
-            @pl.when(z < NZ - 1)
+            @pl.when(z + x_lo < NZ)
             def _():
-                pl.semaphore_wait(ready_sem, NZ - 1 - z)
+                pl.semaphore_wait(ready_sem.at[1], NZ - z - x_lo)
 
         for d in range(1, NZ):
             pl.when(((z + d) % NZ) // (NZ // 2) == part)(z_copies[d - 1].start)
@@ -566,7 +608,7 @@
             pltpu.VMEM((FEAT, COLS), BF16),
             pltpu.VMEM((FEAT, COLS), F32),
             pltpu.VMEM((4, 8, HD), F32),
-            pltpu.SemaphoreType.REGULAR,
+            pltpu.SemaphoreType.REGULAR((3,)),
             dma((2,)),
             dma((8,)),
             dma((2,)),

time: 61.2 us -> 60.7 us (level)
  no operation moved by 1% of the time
where the time goes in v5:
time: 60.7 us; the launch traced here: 60.6 us
  Pallas kernels  59.4 us (98%)
  between operations  1.29 us (2%)
    pallas_call x1, Pallas kernels, local(): pl.pallas_call(kernel, name='diloco_step', out_shape=(jax.ShapeDtypeStruc...  57.3 us
    pallas_call x1, Pallas kernels, local(): pl.pallas_call(update, name='adam_blend', out_shape=(jax.ShapeDtypeStruct...  2.08 us

profile of v5, /device:TPU:1, one launch (start us, length us, event | category | flops | bytes accessed | tf_op | source)
XLA Modules:
  0.0 60.6 jit_solution(9316631863972765576)
XLA Ops:
  1.3 57.3 %diloco_step.1 = (f32[2,4,256,256]{3,2,1,0:T(8,128)S(1)}, f32[2,4,256,256]{3,2,1,0:T(8,128)S(1)}, f32[8,128]{1,0:T(8,128)S(1)}, f32[1024,512]{1,0:T(8,128)S(1)},...) custom-call(bf16[1,1024,512]{2,1,0:T(8,128)(2,1)} %weight.1, ...), custom_call_target="tpu_custom_call" | custom-call | tf_op jit(solution)/shard_map/diloco_step/pallas_call | solution.py:568
  58.6 2.1 %adam_blend.1 = (bf16[1,1024,512]{2,1,0:T(8,128)(2,1)}, f32[1024,512]{1,0:T(8,128)}) custom-call(f32[2,4,256,256]{3,2,1,0:T(8,128)S(1)} %get-tuple-element.10.linear, f32[2,4,256,256]{3,2,1,0:T(8,128)S(1)} %get-tuple-element.11.square, f32[8,128]{1,0:T(8,128)S(1)} %get-tuple-element.12.total_squares, f32[1024,512]{1,0:T(8,128)S(1)} %get-tuple-element.13.level, ...), custom_call_target="tpu_custom_call" | custom-call | tf_op jit(solution)/shard_map/adam_blend/pallas_call | solution.py:641

commit v6 on v5

--- a/solution.py
+++ b/solution.py
@@ -551,11 +551,14 @@
                     result[rows, c : c + HD] = (level[rows, c : c + HD] - speed * step).astype(BF16)
             return 0
 
-        lax.fori_loop(0, PROWS // 16, adam, 0, unroll=4)
-        block = pl.ds(i * PROWS, PROWS)
-        copy = pltpu.make_async_copy(result.at[block], new_weight.at[0, block], weight_sem.at[i])
-        copy.start()
-        copies.append(copy)
+        for h in range(2):
+            lax.fori_loop(h * (PROWS // 32), (h + 1) * (PROWS // 32), adam, 0, unroll=8)
+            block = pl.ds(i * PROWS + h * (PROWS // 2), PROWS // 2)
+            copy = pltpu.make_async_copy(
+                result.at[block], new_weight.at[0, block], weight_sem.at[2 * i + h]
+            )
+            copy.start()
+            copies.append(copy)
     for copy in copies:
         copy.wait()
     momentum_copy.wait()
@@ -647,7 +650,7 @@
         ),
         in_specs=[vmem] * 8,
         out_specs=(any_space, any_space),
-        scratch_shapes=[pltpu.VMEM((FEAT, COLS), BF16), dma((PARTS,)), dma],
+        scratch_shapes=[pltpu.VMEM((FEAT, COLS), BF16), dma((2 * PARTS,)), dma],
         compiler_params=pltpu.CompilerParams(vmem_limit_bytes=16 * 2**20),
     )(*parts)
 

time: 60.7 us -> 60.5 us (level)
  no operation moved by 1% of the time
where the time goes in v6:
time: 60.5 us; the launch traced here: 60.4 us
  Pallas kernels  59.1 us (98%)
  between operations  1.29 us (2%)
    pallas_call x1, Pallas kernels, local(): pl.pallas_call(kernel, name='diloco_step', out_shape=(jax.ShapeDtypeStruc...  57.3 us
    pallas_call x1, Pallas kernels, local(): pl.pallas_call(update, name='adam_blend', out_shape=(jax.ShapeDtypeStruct...  1.83 us

profile of v6, /device:TPU:1, one launch (start us, length us, event | category | flops | bytes accessed | tf_op | source)
XLA Modules:
  0.0 60.4 jit_solution(18112120388494536780)
XLA Ops:
  1.3 57.3 %diloco_step.1 = (f32[2,4,256,256]{3,2,1,0:T(8,128)S(1)}, f32[2,4,256,256]{3,2,1,0:T(8,128)S(1)}, f32[8,128]{1,0:T(8,128)S(1)}, f32[1024,512]{1,0:T(8,128)S(1)},...) custom-call(bf16[1,1024,512]{2,1,0:T(8,128)(2,1)} %weight.1, ...), custom_call_target="tpu_custom_call" | custom-call | tf_op jit(solution)/shard_map/diloco_step/pallas_call | solution.py:571
  58.6 1.8 %adam_blend.1 = (bf16[1,1024,512]{2,1,0:T(8,128)(2,1)}, f32[1024,512]{1,0:T(8,128)}) custom-call(f32[2,4,256,256]{3,2,1,0:T(8,128)S(1)} %get-tuple-element.10.linear, f32[2,4,256,256]{3,2,1,0:T(8,128)S(1)} %get-tuple-element.11.square, f32[8,128]{1,0:T(8,128)S(1)} %get-tuple-element.12.total_squares, f32[1024,512]{1,0:T(8,128)S(1)} %get-tuple-element.13.level, ...), custom_call_target="tpu_custom_call" | custom-call | tf_op jit(solution)/shard_map/adam_blend/pallas_call | solution.py:644
